TPU v7x, 256 devices: a whole 4x4x8 slice. The times are simulated.
256 devices in a mesh: los: 32 (over x, z), sky: 8 (over y, core).
Axes of the slice: x: 4, y: 4, z: 8, core: 2. Of those that a mesh axis runs over, the one named last changes fastest.
Arguments:
- potentials: bfloat16 [128, 128, 4096], P('los', 'sky'), may hold values from -6 to 6
- shell_weight: float32 [128], P('los'), may hold values from 0.004 to 0.02
- shell_dist: float32 [128], P('los'), may hold values from 1 to 6.12, as said below
- source_dist: float32 [128], P('los'), may hold values from 1 to 6.12, as said below
Outputs:
- convergence: bfloat16 [128, 128, 4096], P('los', 'sky')
- shear_one: bfloat16 [128, 128, 4096], P('los', 'sky')
- shear_two: bfloat16 [128, 128, 4096], P('los', 'sky')
Inputs may be any that keep to these rules, and one draw needn't show every extreme that they name: shell_dist rises strictly with the shell index. source_dist[s] lies strictly between shell_dist[s] and shell_dist[s + 1].
All inputs are finite; a program needn't handle non-finite values.
Results may differ from a plain program's by a relative error of at most 0.001.
Values may be sent and summed in bfloat16 or wider, within the bound.
No kernel may reach another device: no remote copies, remote signals or barrier semaphores. Data moves between devices by JAX's collectives and lax.ppermute only.
A program may use at most 64 MiB of HBM per device.

v0:
```python
import jax
import jax.numpy as jnp
from jax import lax
from jax.sharding import PartitionSpec as P


def with_halo(cells, sides, width):
    for axis, dim in sides:
        count = lax.axis_size(axis)
        head = lax.slice_in_dim(cells, 0, width, axis=dim)
        tail = lax.slice_in_dim(cells, cells.shape[dim] - width, cells.shape[dim], axis=dim)
        cells = jnp.concatenate(
            [
                lax.ppermute(tail, axis, [(i, (i + 1) % count) for i in range(count)]),
                cells,
                lax.ppermute(head, axis, [((i + 1) % count, i) for i in range(count)]),
            ],
            axis=dim,
        )
    return cells


def first_cols(field):
    return (
        jnp.roll(field, 2, axis=-1)
        - 8.0 * jnp.roll(field, 1, axis=-1)
        + 8.0 * jnp.roll(field, -1, axis=-1)
        - jnp.roll(field, -2, axis=-1)
    ) / 12.0


def second_cols(field):
    return (
        -jnp.roll(field, 2, axis=-1)
        + 16.0 * jnp.roll(field, 1, axis=-1)
        - 30.0 * field
        + 16.0 * jnp.roll(field, -1, axis=-1)
        - jnp.roll(field, -2, axis=-1)
    ) / 12.0


def first_rows(padded, height):
    return (
        padded[:, 0:height, :]
        - 8.0 * padded[:, 1 : height + 1, :]
        + 8.0 * padded[:, 3 : height + 3, :]
        - padded[:, 4 : height + 4, :]
    ) / 12.0


def second_rows(padded, height):
    return (
        -padded[:, 0:height, :]
        + 16.0 * padded[:, 1 : height + 1, :]
        - 30.0 * padded[:, 2 : height + 2, :]
        + 16.0 * padded[:, 3 : height + 3, :]
        - padded[:, 4 : height + 4, :]
    ) / 12.0


def local_sums(potential, near_weight, far_weight):
    field = potential.astype(jnp.float32)
    local_near = jnp.cumsum(near_weight[:, None, None] * field, axis=0)
    local_far = jnp.cumsum(far_weight[:, None, None] * field, axis=0)
    return (local_near, local_far)


def nearer_sums(total_near, total_far):
    stacked = jnp.stack((total_near, total_far))[None]
    received = lax.all_to_all(stacked, "los", split_axis=3, concat_axis=0, tiled=True)
    earlier = jnp.cumsum(received, axis=0) - received
    result = lax.all_to_all(earlier, "los", split_axis=0, concat_axis=3, tiled=True)
    return (result[0, 0], result[0, 1])


def lens_from(local_near, local_far, prefix, source_dist):
    running_near = prefix[0][None] + local_near
    running_far = prefix[1][None] + local_far
    return running_near - running_far / source_dist[:, None, None]


def on_device(potentials, shell_weight, shell_dist, source_dist):
    height = potentials.shape[1]
    near_weight = shell_weight * shell_dist
    far_weight = near_weight * shell_dist
    local_near, local_far = local_sums(potentials, near_weight, far_weight)
    prefix = nearer_sums(local_near[-1], local_far[-1])
    lens_map = lens_from(local_near, local_far, prefix, source_dist)
    padded = with_halo(lens_map, (("sky", 1),), 2)
    interior = padded[:, 2 : height + 2, :]
    second_x = second_cols(interior)
    second_y = second_rows(padded, height)
    cross = first_rows(first_cols(padded), height)
    convergence = (0.5 * (second_x + second_y)).astype(jnp.bfloat16)
    shear_one = (0.5 * (second_x - second_y)).astype(jnp.bfloat16)
    shear_two = cross.astype(jnp.bfloat16)
    return (convergence, shear_one, shear_two)


def solution(mesh):
    return jax.shard_map(
        on_device,
        mesh=mesh,
        in_specs=(P("los", "sky", None), P("los"), P("los"), P("los")),
        out_specs=(P("los", "sky", None), P("los", "sky", None), P("los", "sky", None)),
        check_vma=False,
    )
```

profile of v0, /device:TPU:32, one launch (start us, length us, event | category | flops | bytes accessed | tf_op | source)
XLA Modules:
  0.0 103.1 jit_solution(17439832646547839495)
XLA Ops:
  0.6 0.7 fusion.27
  1.4 1.2 %fusion.2 = f32[4,16,4096]{2,1,0:T(8,128)S(1)} fusion(bf16[4,16,4096]{2,1,0:T(8,128)(2,1)} %param.4, f32[4]{0:T(128)S(1)} %get-tuple-element.15), kind=kOutput, calls=%fused_computation.15 | output fusion | flops 1310720 | bytes 1572880 | tf_op jit(solution)/shard_map/jit(cumsum)/reduce_window_sum | solution.py:64
  2.6 0.2 fusion.1
  2.9 4.4 %copy.83 = f32[1,2,16,4096]{2,1,0,3:T(2,128)} copy(f32[1,2,16,4096]{3,2,1,0:T(8,128)S(1)} %maximum_bitcast_fusion) | data formatting | bytes 1048576 | tf_op jit(solution)/shard_map/broadcast_in_dim | solution.py:69
  7.2 7.3 %reshape.11 = f32[32,1,4096]{2,1,0:T(1,128)S(1)} reshape(f32[4096,1,2,16]{3,2,1,0:T(2,128)} %bitcast.18) | data formatting | bytes 1048576
  14.6 28.6 %all_to_all.36 = f32[32,1,4096]{2,1,0:T(1,128)S(1)} all-to-all(f32[32,1,4096]{2,1,0:T(1,128)S(1)} %reshape.11), channel_id=1, replica_groups=mesh['los'=32,'sky'=8] {'los'}, dimensions={0} | all-to-all | bytes 1048576 | tf_op jit(solution)/shard_map/all_to_all | solution.py:70
  43.2 0.5 broadcast.48
  43.7 1.9 %reduce = f32[32,4096]{1,0:T(8,128)S(1)} reduce(f32[32,1,4096]{2,1,0:T(1,128)S(1)} %all_to_all.36, f32[]{:T(128)} %broadcast.48), dimensions={1}, to_apply=%all_to_all.26.reduce_sub_computation | reduce | bytes 1048580 | tf_op jit(solution)/shard_map/all_to_all | solution.py:70
  45.6 6.9 %reshape.12 = f32[4096,1,2,16]{3,2,1,0:T(2,128)} reshape(f32[32,4096]{1,0:T(8,128)S(1)} %reduce) | data formatting | bytes 1048576
  52.5 5.1 %copy.85 = f32[1,2,16,32,128]{4,2,1,3,0:T(8,128)S(1)} copy(f32[1,2,16,32,128]{2,1,4,3,0:T(2,128)} %bitcast.19) | data formatting | bytes 1048576 | tf_op jit(solution)/shard_map/all_to_all | solution.py:70
  57.6 4.1 %reduce-window_subtract_fusion = f32[32,2,16,128]{3,2,1,0:T(8,128)S(1)} fusion(f32[1,2,16,32,128]{4,2,1,3,0:T(8,128)S(1)} %copy.85), kind=kOutput, calls=%fused_computation.47 | output fusion | flops 4194304 | bytes 1048576 | tf_op jit(solution)/shard_map/jit(cumsum)/reduce_window_sum | solution.py:71
  61.7 21.6 %all_to_all.37 = f32[32,2,16,128]{3,2,1,0:T(8,128)S(1)} all-to-all(f32[32,2,16,128]{3,2,1,0:T(8,128)S(1)} %reduce-window_subtract_fusion), channel_id=1, replica_groups=mesh['los'=32,'sky'=8] {'los'}, dimensions={0} | all-to-all | bytes 1048576 | tf_op jit(solution)/shard_map/all_to_all | solution.py:72
  83.3 0.3 copy.86
  83.7 0.3 copy_bitcast_fusion
  84.0 0.3 copy-done.1
  84.3 0.3 divide_subtract_fusion
  84.8 0.4 fusion.33
  85.1 0.4 fusion.35
  85.7 0.5 collective-permute-start
  86.3 5.2 %collective-permute-done = f32[4,2,4096]{2,0,1:T(4,128)S(1)} collective-permute-done((f32[4,2,4096]{2,0,1:T(4,128)S(1)}, f32[4,2,4096]{2,0,1:T(4,128)S(1)}, u32[]{:S(2)}, u32[]{:S(2)}) %collective-permute-start) | collective-permute-done | bytes 131104 | tf_op jit(solution)/shard_map/ppermute | solution.py:14
  91.5 0.7 copy_dynamic-update-slice_fusion
  92.4 0.8 fusion.31
  93.2 0.8 fusion.28
  94.1 0.3 pad_maximum_fusion.1
  94.4 0.4 pad_maximum_fusion
  94.8 1.4 %maximum_subtract_fusion = f32[4,20,4096]{2,0,1:T(4,128)S(1)} fusion(f32[4,20,4094]{2,0,1:T(4,128)S(1)} %get-tuple-element.23, f32[4,20,2]{2,0,1:T(4,128)S(1)} %get-tuple-element.21, f32[4,20,4095]{2,0,1:T(4,128)S(1)} %get-tuple-element.18, f32[4,20,1]{2,0,1:T(4,128)S(1)} %get-tuple-element.20), kind=kLoop, calls=%fused_computation.10 | loop fusion | flops 1310720 | bytes 3932160 | tf_op jit(solution)/shard_map/sub | solution.py:25
  96.2 2.3 %fusion = f32[4,20,4096]{2,1,0:T(8,128)S(1)} fusion(f32[4,20,4096]{2,0,1:T(4,128)S(1)} %pad_maximum_fusion.1, f32[4,20,4096]{2,0,1:T(4,128)S(1)} %maximum_subtract_fusion, f32[4,20,4096]{2,0,1:T(4,128)S(1)} %pad_maximum_fusion), kind=kLoop, calls=%fused_computation.5 | loop fusion | flops 1310720 | bytes 5242880 | tf_op jit(solution)/shard_map/div | solution.py:24
  98.5 1.2 %fusion.13 = bf16[4,16,4096]{2,1,0:T(8,128)(2,1)} fusion(f32[4,20,4096]{2,1,0:T(8,128)S(1)} %fusion), kind=kLoop, calls=%fused_computation.27 | loop fusion | flops 1835008 | bytes 4718592 | tf_op jit(solution)/shard_map/convert_element_type | solution.py:96
  99.8 0.1 copy.90
  99.9 0.1 copy.88
  100.0 2.2 %multiply_convert_fusion = (bf16[4,16,4096]{2,1,0:T(8,128)(2,1)}, f32[4,16,4096]{2,1,0:T(8,128)S(1)}, f32[4,16,4096]{2,1,0:T(8,128)S(1)}) fusion(f32[4,2,4096]{2,1,0:T(2,128)S(1)} %copy.90, f32[4,16,4096]{2,1,0:T(8,128)S(1)} %divide_subtract_fusion, f32[4,2,4096]{2,1,0:T(2,128)S(1)} %copy.88, f32[4,16,2]{2,1,0:T(8,128)S(1)} %get-tuple-element.26, ...), kind=kLoop, calls=%fused_computation.44 | loop fusion | flops 7340032 | bytes 8126464 | tf_op jit(solution)/shard_map/convert_element_type | solution.py:95
  102.2 0.9 multiply_convert_fusion.1
  (18 shorter events, 0.8 us)
Async XLA Ops:
  0.6 2.0 %copy-start = (bf16[4,16,4096]{2,1,0:T(8,128)(2,1)S(1)}, bf16[4,16,4096]{2,1,0:T(8,128)(2,1)}, u32[]{:S(2)}) copy-start(bf16[4,16,4096]{2,1,0:T(8,128)(2,1)} %param.4) | copy-start | bytes 1572868
  83.6 0.7 copy-start.1
  85.6 6.7 %collective-permute-start.1 = (f32[4,2,4096]{2,0,1:T(4,128)S(1)}, f32[4,2,4096]{2,0,1:T(4,128)S(1)}, u32[]{:S(2)}, u32[]{:S(2)}) collective-permute-start(f32[4,2,4096]{2,0,1:T(4,128)S(1)} %copy.89), channel_id=1, source_target_pairs={{1,0},{2,1},{3,2},{4,3},{5,4},{6,5},{7,6},{0,7},{9,8},{10,9},{11,1... | collective-permute-start | bytes 393224 | tf_op jit(solution)/shard_map/ppermute | solution.py:16
  85.7 5.8 %collective-permute-start = (f32[4,2,4096]{2,0,1:T(4,128)S(1)}, f32[4,2,4096]{2,0,1:T(4,128)S(1)}, u32[]{:S(2)}, u32[]{:S(2)}) collective-permute-start(f32[4,2,4096]{2,0,1:T(4,128)S(1)} %copy.87), channel_id=1, source_target_pairs={{0,1},{1,2},{2,3},{3,4},{4,5},{5,6},{6,7},{7,0},{8,9},{9,10},{10,1... | collective-permute-start | bytes 393224 | tf_op jit(solution)/shard_map/ppermute | solution.py:14
where the time goes:
time: 103 us
  blocking collectives  50.2 us (49%)
  local copies, waits for them, and re-layouts  29.1 us (28%)
  other arithmetic  17.2 us (17%)
  waiting for transfers between devices  5.2 us (5%)
    all_to_all x1, blocking collectives, nearer_sums(): lax.all_to_all(stacked, 'los', split_axis=3, concat_axis=0, tiled=True)  28.6 us
    all_to_all x1, blocking collectives, nearer_sums(): lax.all_to_all(earlier, 'los', split_axis=0, concat_axis=3, tiled=True)  21.6 us
    unnamed x9, local copies, waits for them, and re-layouts  15.6 us
    all_to_all x2, local copies, waits for them, and re-layouts, nearer_sums(): lax.all_to_all(stacked, 'los', split_axis=3, concat_axis=0, tiled=True)  5.62 us
    ppermute x1, waiting for transfers between devices, with_halo(): lax.ppermute(tail, axis, [(i, (i + 1) % count) for i in range(count)])  5.2 us
    broadcast_in_dim x1, local copies, waits for them, and re-layouts, nearer_sums(): stacked = jnp.stack((total_near, total_far))[None]  4.39 us
    another operation x1, other arithmetic, nearer_sums(): earlier = jnp.cumsum(received, axis=0) - received  4.06 us
    div x1, other arithmetic, first_cols(): (jnp.roll(field, 2, axis=-1) - 8.0 * jnp.roll(field, 1, axis=-1) + 8.0 *...  2.3 us
  transfers between devices with their start and end apart: 2, of which 1 were waited for; matrix products, arithmetic and copies ran while one was open for 1% of the time, Pallas kernels for 0%

commit v1 on v0

--- a/solution.py
+++ b/solution.py
@@ -67,7 +67,10 @@
 
 def nearer_sums(total_near, total_far):
     stacked = jnp.stack((total_near, total_far))[None]
-    received = lax.all_to_all(stacked, "los", split_axis=3, concat_axis=0, tiled=True)
+    received = jnp.concatenate(
+        lax.all_to_all(jnp.stack(jnp.split(stacked, lax.axis_size("los"), axis=3)), "los", 0, 0),
+        axis=0,
+    )
     earlier = jnp.cumsum(received, axis=0) - received
     result = lax.all_to_all(earlier, "los", split_axis=0, concat_axis=3, tiled=True)
     return (result[0, 0], result[0, 1])

time: 103 us -> 74 us (0.72); the launches traced: 103 us -> 72.6 us
  local copies, waits for them, and re-layouts: 29.1 us -> 2.86 us
  other arithmetic: 17.2 us -> 13 us
  waiting for transfers between devices: 5.2 us -> 2.57 us
  starting transfers between devices: 0.52 us -> 2.96 us
    unnamed x9 -> x36, local copies, waits for them, and re-layouts: 15.6 us -> 0.46 us
    all_to_all x2 -> x0, local copies, waits for them, and re-layouts: 5.62 us -> none  [nearer_sums(): lax.all_to_all(stacked, 'los', split_axis=3, concat_axis=0, tiled=True)]
    broadcast_in_dim x1 -> x0, local copies, waits for them, and re-layouts: 4.39 us -> none  [nearer_sums(): stacked = jnp.stack((total_near, total_far))[None]]
    ppermute x1, starting transfers between devices: 0.02 us -> 2.96 us  [with_halo(): lax.ppermute(head, axis, [((i + 1) % count, i) for i in range(count)])]
    ppermute x1, waiting for transfers between devices: 5.2 us -> 2.57 us  [with_halo(): lax.ppermute(tail, axis, [(i, (i + 1) % count) for i in range(count)])]
    all_to_all x1 -> x0, other arithmetic: 1.89 us -> none  [nearer_sums(): lax.all_to_all(stacked, 'los', split_axis=3, concat_axis=0, tiled=True)]
    sub x1 -> x0, other arithmetic: 1.42 us -> none  [first_cols(): jnp.roll(field, 2, axis=-1) - 8.0 * jnp.roll(field, 1, axis=-1)]
    another operation x1, other arithmetic: 1.2 us -> 0.16 us  [local_sums(): local_far = jnp.cumsum(far_weight[:, None, None] * field, axis=0)]
  transfers between devices with their start and end apart: 2 -> 2, of which waited for: 1 -> 1; matrix products, arithmetic and copies ran while one was open for 1% -> 0% of each run, Pallas kernels for 0% -> 0%
where the time goes in v1:
time: 74 us; the launch traced here: 72.6 us
  blocking collectives  50.2 us (68%)
  other arithmetic  13 us (18%)
  starting transfers between devices  2.96 us (4%)
  local copies, waits for them, and re-layouts  2.86 us (4%)
  waiting for transfers between devices  2.57 us (3%)
  between operations  1 us (1%)
    all_to_all x1, blocking collectives, nearer_sums(): lax.all_to_all(jnp.stack(jnp.split(stacked, lax.axis_size('los'), axis=3)...  28.6 us
    all_to_all x1, blocking collectives, nearer_sums(): lax.all_to_all(earlier, 'los', split_axis=0, concat_axis=3, tiled=True)  21.6 us
    another operation x1, other arithmetic, nearer_sums(): earlier = jnp.cumsum(received, axis=0) - received  3.97 us
    ppermute x1, starting transfers between devices, with_halo(): lax.ppermute(head, axis, [((i + 1) % count, i) for i in range(count)])  2.96 us
    ppermute x1, waiting for transfers between devices, with_halo(): lax.ppermute(tail, axis, [(i, (i + 1) % count) for i in range(count)])  2.57 us
    convert_element_type x1, other arithmetic, on_device(): shear_one = (0.5 * (second_x - second_y)).astype(jnp.bfloat16)  2.22 us
    div x1, other arithmetic, first_cols(): (jnp.roll(field, 2, axis=-1) - 8.0 * jnp.roll(field, 1, axis=-1) + 8.0 *...  2.01 us
  transfers between devices with their start and end apart: 2, of which 1 were waited for; matrix products, arithmetic and copies ran while one was open for 0% of the time, Pallas kernels for 0%

profile of v1, /device:TPU:32, one launch (start us, length us, event | category | flops | bytes accessed | tf_op | source)
XLA Modules:
  0.0 72.6 jit_solution(3506243648050748723)
XLA Ops:
  0.6 0.0 copy-start
  0.6 0.7 %fusion.36 = (f32[4]{0:T(128)S(1)}, f32[4]{0:T(128)S(1)}) fusion(f32[4]{0:T(128)} %param.6, f32[4]{0:T(128)} %param.5), kind=kLoop, calls=%fused_computation.128 | loop fusion | flops 8 | bytes 64 | tf_op jit(solution)/shard_map/mul | solution.py:88
  1.4 1.2 %fusion.10 = f32[4,16,4096]{2,1,0:T(8,128)S(1)} fusion(bf16[4,16,4096]{2,1,0:T(8,128)(2,1)} %param.4, f32[4]{0:T(128)S(1)} %get-tuple-element.7), kind=kOutput, calls=%fused_computation.25 | output fusion | flops 1310720 | bytes 1572880 | tf_op jit(solution)/shard_map/jit(cumsum)/reduce_window_sum | solution.py:63
  2.6 0.0 copy-done
  2.6 0.2 fusion.11
  2.8 0.1 maximum_bitcast_fusion
  3.3 28.6 %all_to_all.23 = f32[32,1,2,16,128]{4,3,2,1,0:T(8,128)S(1)} all-to-all(f32[32,1,2,16,128]{4,3,2,1,0:T(8,128)S(1)} %constant_dynamic-update-slice_fusion), channel_id=1, replica_groups=mesh['los'=32,'sky'=8] {'los'}, dimensions={0} | all-to-all | bytes 1048576 | tf_op jit(solution)/shard_map/all_to_all | solution.py:71
  31.9 4.0 %reduce-window_subtract_fusion = f32[32,2,16,128]{3,2,1,0:T(8,128)S(1)} fusion(f32[32,1,2,16,128]{4,3,2,1,0:T(8,128)S(1)} %all_to_all.23), kind=kOutput, calls=%fused_computation.57 | output fusion | flops 4194304 | bytes 1048576 | tf_op jit(solution)/shard_map/jit(cumsum)/reduce_window_sum | solution.py:74
  35.9 21.6 %all_to_all.24 = f32[32,2,16,128]{3,2,1,0:T(8,128)S(1)} all-to-all(f32[32,2,16,128]{3,2,1,0:T(8,128)S(1)} %reduce-window_subtract_fusion), channel_id=1, replica_groups=mesh['los'=32,'sky'=8] {'los'}, dimensions={0} | all-to-all | bytes 1048576 | tf_op jit(solution)/shard_map/all_to_all | solution.py:75
  57.5 0.0 copy-start.1
  57.5 0.3 copy.70
  57.8 0.3 copy_bitcast_fusion
  58.1 0.0 copy-done.1
  58.1 0.3 divide_subtract_fusion
  58.4 0.1 fusion.43
  58.5 0.3 fusion.40
  58.9 0.4 fusion.42
  59.3 0.1 fusion.39
  59.3 0.0 collective-permute-start
  59.3 3.0 %collective-permute-start.1 = (f32[4,2,4096]{2,1,0:T(2,128)S(1)}, f32[4,2,4096]{2,1,0:T(2,128)S(1)}, u32[]{:S(2)}, u32[]{:S(2)}) collective-permute-start(f32[4,2,4096]{2,1,0:T(2,128)S(1)} %get-tuple-element.21), channel_id=1, source_target_pairs={{1,0},{2,1},{3,2},{4,3},{5,4},{6,5},{7,6},{0,7},{9,8},{10,9},{11,1... | collective-permute-start | bytes 393224 | tf_op jit(solution)/shard_map/ppermute | solution.py:16
  62.3 0.1 fusion.41
  62.4 2.6 %collective-permute-done = f32[4,2,4096]{2,1,0:T(2,128)S(1)} collective-permute-done((f32[4,2,4096]{2,1,0:T(2,128)S(1)}, f32[4,2,4096]{2,1,0:T(2,128)S(1)}, u32[]{:S(2)}, u32[]{:S(2)}) %collective-permute-start) | collective-permute-done | bytes 131104 | tf_op jit(solution)/shard_map/ppermute | solution.py:14
  64.9 0.0 collective-permute-done.1
  64.9 0.2 pad_maximum_fusion.8
  65.2 0.5 fusion.38
  65.7 0.5 fusion.37
  66.2 2.0 %fusion.2 = f32[4,20,4096]{2,1,0:T(8,128)S(1)} fusion(f32[4,2,4096]{2,1,0:T(2,128)S(1)} %collective-permute-done.1, f32[4,16,4096]{2,1,0:T(8,128)S(1)} %divide_subtract_fusion, f32[4,2,4096]{2,1,0:T(2,128)S(1)} %collective-permute-done, f32[4,20,4094]{2,1,0:T(8,128)S(1)} %get-tuple-element.9, f32[4,20,4095]{2,1,0:T(8,128)S(1)} %get-tuple-element.11, ...), kind=kLoop, calls=%fused_computation.3 | loop fusion | flops 5898240 | bytes 7862400 | tf_op jit(solution)/shard_map/div | solution.py:24
  68.3 1.2 %fusion.22 = bf16[4,16,4096]{2,1,0:T(8,128)(2,1)} fusion(f32[4,20,4096]{2,1,0:T(8,128)S(1)} %fusion.2), kind=kLoop, calls=%fused_computation.38 | loop fusion | flops 1835008 | bytes 4718592 | tf_op jit(solution)/shard_map/convert_element_type | solution.py:99
  69.5 2.2 %multiply_convert_fusion = (bf16[4,16,4096]{2,1,0:T(8,128)(2,1)}, f32[4,16,4096]{2,1,0:T(8,128)S(1)}, f32[4,16,4096]{2,1,0:T(8,128)S(1)}) fusion(f32[4,2,4096]{2,1,0:T(2,128)S(1)} %collective-permute-done.1, f32[4,16,4096]{2,1,0:T(8,128)S(1)} %divide_subtract_fusion, f32[4,2,4096]{2,1,0:T(2,128)S(1)} %collective-permute-done, ...), kind=kLoop, calls=%fused_computation.54 | loop fusion | flops 7340032 | bytes 8126464 | tf_op jit(solution)/shard_map/convert_element_type | solution.py:98
  71.7 0.9 %multiply_convert_fusion.1 = bf16[4,16,4096]{2,1,0:T(8,128)(2,1)} fusion(f32[4,16,4096]{2,1,0:T(8,128)S(1)} %get-tuple-element.5, f32[4,16,4096]{2,1,0:T(8,128)S(1)} %get-tuple-element.4), kind=kLoop, calls=%fused_computation.55 | loop fusion | flops 786432 | bytes 2621440 | tf_op jit(solution)/shard_map/convert_element_type | solution.py:97
  (35 shorter events, 0.2 us)
Async XLA Ops:
  0.6 2.0 %copy-start = (bf16[4,16,4096]{2,1,0:T(8,128)(2,1)S(1)}, bf16[4,16,4096]{2,1,0:T(8,128)(2,1)}, u32[]{:S(2)}) copy-start(bf16[4,16,4096]{2,1,0:T(8,128)(2,1)} %param.4) | copy-start | bytes 1572868
  57.5 0.7 copy-start.1
  59.3 5.6 %collective-permute-start = (f32[4,2,4096]{2,1,0:T(2,128)S(1)}, f32[4,2,4096]{2,1,0:T(2,128)S(1)}, u32[]{:S(2)}, u32[]{:S(2)}) collective-permute-start(f32[4,2,4096]{2,1,0:T(2,128)S(1)} %get-tuple-element.20), channel_id=1, source_target_pairs={{0,1},{1,2},{2,3},{3,4},{4,5},{5,6},{6,7},{7,0},{8,9},{9,10},{10,1... | collective-permute-start | bytes 393224 | tf_op jit(solution)/shard_map/ppermute | solution.py:14
  59.3 5.6 %collective-permute-start.1 = (f32[4,2,4096]{2,1,0:T(2,128)S(1)}, f32[4,2,4096]{2,1,0:T(2,128)S(1)}, u32[]{:S(2)}, u32[]{:S(2)}) collective-permute-start(f32[4,2,4096]{2,1,0:T(2,128)S(1)} %get-tuple-element.21), channel_id=1, source_target_pairs={{1,0},{2,1},{3,2},{4,3},{5,4},{6,5},{7,6},{0,7},{9,8},{10,9},{11,1... | collective-permute-start | bytes 393224 | tf_op jit(solution)/shard_map/ppermute | solution.py:16
